TPU v7x, 256 devices: a whole 4x4x8 slice. The times are simulated.
256 devices in a mesh: rows: 8 (over z), hidden: 32 (over x, y, core).
Axes of the slice: x: 4, y: 4, z: 8, core: 2. Of those that a mesh axis runs over, the one named last changes fastest.
Arguments:
- tokens: bfloat16 [1024, 8192], P('hidden', 'rows'), may hold values from -6 to 6
- snapshot: int32 [1024, 1], replicated, may hold values from 0 to 63; in each aligned block of 1024 rows (0 to 1023, 1024 to 2047, ...) at most 32 rows name the same one
- gate_weight: bfloat16 [8192, 28672], P('rows', 'hidden'), may hold values from -0.0625 to 0.0625
- up_weight: bfloat16 [8192, 28672], P('rows', 'hidden'), may hold values from -0.0625 to 0.0625
- down_weight: bfloat16 [28672, 8192], P('hidden', 'rows'), may hold values from -0.03125 to 0.03125
- adapter_input_maps: bfloat16 [64, 8192, 128], P('hidden', 'rows')
- adapter_middle_maps: bfloat16 [64, 2, 64, 28672], P(None, None, 'rows', 'hidden'), may hold values from -0.375 to 0.375
- down_input_map: bfloat16 [64, 64, 28672], P(None, 'rows', 'hidden')
- down_output_map: bfloat16 [64, 64, 8192], P('hidden', None, 'rows'), may hold values from -0.75 to 0.75
Outputs:
- mixed: bfloat16 [1024, 8192], P('hidden', 'rows')
Inputs may be any that keep to these rules, and one draw needn't show every extreme that they name: Every snapshot is named by at least one row and by at most 32 rows; some snapshot is named by exactly 32 rows.
All inputs are finite; a program needn't handle non-finite values.
Results may differ from a plain program's by a relative error of at most 0.033.
Values may be sent and summed in bfloat16 or wider, within the bound.
No kernel may reach another device: no remote copies, remote signals or barrier semaphores. Data moves between devices by JAX's collectives and lax.ppermute only.
A program may use at most 128 MiB of HBM per device.

v0:
```python
import jax
import jax.numpy as jnp
from jax import lax
from jax.sharding import PartitionSpec as P


def slot_tables(snapshot, snapshot_total, capacity):
    row_total = snapshot.shape[0]
    snap_owner = snapshot[:, 0]
    onehot = (snap_owner[:, None] == jnp.arange(snapshot_total, dtype=jnp.int32)[None, :]).astype(
        jnp.int32
    )
    before = jnp.cumsum(onehot, axis=0) - onehot
    slot_index = jnp.sum(before * onehot, axis=1)
    token_of = jnp.full((snapshot_total, capacity), row_total, jnp.int32)
    token_of = token_of.at[snap_owner, slot_index].set(jnp.arange(row_total, dtype=jnp.int32))
    return (snap_owner, slot_index, token_of)


def swiglu(paired):
    return (jax.nn.silu(paired[:, 0]) * paired[:, 1]).astype(jnp.bfloat16)


def per_device(
    tokens,
    snapshot,
    gate_weight,
    up_weight,
    down_weight,
    adapter_input_maps,
    adapter_middle_maps,
    down_input_map,
    down_output_map,
):
    row_index = lax.axis_index("rows")
    hidden_index = lax.axis_index("hidden")
    all_count = snapshot.shape[0]
    snapshot_total = adapter_middle_maps.shape[0]
    capacity = 2 * all_count // snapshot_total
    snapshot_local = adapter_input_maps.shape[0]
    rank_block_values = adapter_middle_maps.shape[2]
    rank_full = down_output_map.shape[1]
    snap_owner, slot_index, token_of = slot_tables(snapshot, snapshot_total, capacity)
    filled_flag = token_of < all_count
    clamped_index = jnp.minimum(token_of, all_count - 1)
    own_first = hidden_index * snapshot_local
    own_clamped = lax.dynamic_slice_in_dim(clamped_index, own_first, snapshot_local, 0)
    own_filled = lax.dynamic_slice_in_dim(filled_flag, own_first, snapshot_local, 0)
    own_tokens = lax.dynamic_slice_in_dim(token_of, own_first, snapshot_local, 0)
    gathered = lax.all_gather(tokens, "hidden", axis=0, tiled=True)
    picked_snapshot = jnp.where(
        own_filled[:, :, None], gathered[own_clamped], jnp.zeros((), gathered.dtype)
    )
    rank_partial_values = jnp.einsum(
        "leh,lhr->ler", picked_snapshot, adapter_input_maps, preferred_element_type=jnp.float32
    )
    rank_partial_values = rank_partial_values.reshape(snapshot_local, capacity, 2, rank_full)
    placed = jnp.zeros((snapshot_total, capacity, 2, rank_full), jnp.float32)
    placed = lax.dynamic_update_slice_in_dim(placed, rank_partial_values, own_first, 0)
    rank_total = lax.psum(placed, ("rows", "hidden"))
    rank_activation_values = lax.dynamic_slice_in_dim(
        rank_total, row_index * rank_block_values, rank_block_values, 3
    ).astype(jnp.bfloat16)
    halves = []
    for half_position in range(2):
        grouped_rows = jnp.einsum(
            "sck,skf->scf",
            rank_activation_values[:, :, half_position],
            adapter_middle_maps[:, half_position],
            preferred_element_type=jnp.float32,
        )
        halves.append(grouped_rows[snap_owner, slot_index])
    adapter_gate_up = jnp.stack(halves, axis=1)
    gate_term = jnp.dot(gathered, gate_weight, preferred_element_type=jnp.float32)
    up_term = jnp.dot(gathered, up_weight, preferred_element_type=jnp.float32)
    adapter_rows = adapter_gate_up
    summed = lax.psum(
        (jnp.stack([gate_term, up_term], axis=1) + adapter_rows).astype(jnp.bfloat16), "rows"
    ).astype(jnp.float32)
    hidden_all = swiglu(summed)
    rows_grouped = jnp.where(
        filled_flag[:, :, None], hidden_all[clamped_index], jnp.zeros((), hidden_all.dtype)
    )
    down_part = jnp.einsum(
        "scf,skf->sck", rows_grouped, down_input_map, preferred_element_type=jnp.float32
    )
    placed_down = jnp.zeros((snapshot_total, capacity, rank_full), jnp.float32)
    placed_down = lax.dynamic_update_slice_in_dim(
        placed_down, down_part, row_index * rank_block_values, 2
    )
    down_total = lax.psum(placed_down, ("rows", "hidden"))
    down_rank = lax.dynamic_slice_in_dim(down_total, own_first, snapshot_local, 0).astype(
        jnp.bfloat16
    )
    lifted = jnp.einsum(
        "sck,skd->scd", down_rank, down_output_map, preferred_element_type=jnp.float32
    )
    feature_width = lifted.shape[2]
    adapter_down = jnp.zeros((all_count + 1, feature_width), jnp.float32)
    adapter_down = adapter_down.at[own_tokens.reshape(-1)].add(lifted.reshape(-1, feature_width))[
        :all_count
    ]
    adapter_rows = adapter_down
    return lax.psum_scatter(
        (
            jnp.dot(hidden_all, down_weight, preferred_element_type=jnp.float32) + adapter_rows
        ).astype(jnp.bfloat16),
        "hidden",
        scatter_dimension=0,
        tiled=True,
    )


def solution(mesh):
    return jax.shard_map(
        per_device,
        mesh=mesh,
        in_specs=(
            P("hidden", "rows"),
            P(),
            P("rows", "hidden"),
            P("rows", "hidden"),
            P("hidden", "rows"),
            P("hidden", "rows", None),
            P(None, None, "rows", "hidden"),
            P(None, "rows", "hidden"),
            P("hidden", None, "rows"),
        ),
        out_specs=P("hidden", "rows"),
        check_vma=False,
    )
```

profile of v0, /device:TPU:2, one launch (start us, length us, event | category | flops | bytes accessed | tf_op | source)
XLA Modules:
  0.0 571.1 jit_solution(12695949925899009694)
XLA Ops:
  6.5 0.7 all-gather.2.cloned.1.call-update
  7.3 0.7 fusion.19
  8.0 18.0 %reduce-window.6 = s32[64,8,128]{2,1,0:T(8,128)S(1)} reduce-window(s32[64,8,128]{2,1,0:T(8,128)S(1)} %fusion.19, s32[]{:T(128)} %constant.16.clone.1), window={size=1x1x128 pad=0_0x0_0x127_0}, to_apply=%region_0.0 | reduce-window | flops 8323072 | bytes 524292 | tf_op jit(solution)/shard_map/reduce-window
  26.0 0.1 slice.44
  26.2 0.1 copy.13
  26.4 0.1 copy.14
  26.4 0.1 broadcast_add_fusion
  26.6 0.8 fusion.18
  27.3 0.7 shift-left_or_fusion
  28.1 0.7 multiply_reduce_fusion
  28.8 0.8 and_reduce_fusion
  29.6 4.3 scatter_custom_fusion.1
  34.1 0.1 copy.16
  34.1 0.1 reshape.78
  34.3 0.1 copy.15
  34.4 26.9 %all-gather.2.cloned.1.call-done = bf16[1024,1024]{1,0:T(8,128)(2,1)} async-done(((bf16[32,1024]{1,0:T(8,128)(2,1)}), bf16[1024,1024]{1,0:T(8,128)(2,1)}) %all-gather.2.cloned.1.call-update) | async-done | bytes 2097168 | tf_op jit(solution)/shard_map/all_gather | solution.py:50
  61.4 2.7 gather_fusion
  64.0 0.3 fusion.20
  64.3 0.1 reshape.69
  64.4 0.1 copy.17
  64.5 2.5 broadcast_in_dim.49
  67.0 0.6 constant_dynamic-update-slice_fusion
  67.6 130.6 %all-reduce.5 = bf16[64,32,2,64]{1,3,0,2:T(8,128)(2,1)} all-reduce(f32[64,32,2,64]{1,3,0,2:T(8,128)} %constant_dynamic-update-slice_fusion), channel_id=1, replica_groups=mesh['rows'=8,'hidden'=32] {'rows','hidden'}, use_global_device_ids=true, to_apply=%region_4.5 | all-reduce | flops 262144 | bytes 1572864 | tf_op jit(solution)/shard_map/psum | solution.py:60
  198.2 1.0 dynamic-slice_convert_fusion
  199.2 5.5 fusion.12
  204.7 4.1 fusion.10
  208.8 19.8 %gather_fusion.1 = f32[1024,896]{1,0:T(8,128)} fusion(f32[64,32,896]{2,1,0:T(8,128)} %fusion.12, s32[1024]{0:T(1024)S(1)} %bitcast.78), kind=kCustom, calls=%fused_computation.1 | custom fusion | bytes 7348224 | tf_op jit(solution)/shard_map/gather | solution.py:72
  228.7 19.9 %gather_fusion.2 = f32[1024,896]{1,0:T(8,128)} fusion(f32[64,32,896]{2,1,0:T(8,128)} %fusion.10, s32[1024]{0:T(1024)S(1)} %bitcast.79), kind=kCustom, calls=%fused_computation.2 | custom fusion | bytes 7348224 | tf_op jit(solution)/shard_map/gather | solution.py:72
  248.5 4.6 convolution_bitcast_fusion
  253.2 2.3 convolution_bitcast_fusion.1
  255.5 0.8 copy-done.2
  256.3 2.1 fusion
  258.5 0.2 reduce-scatter.2.cloned.1.call-start
  258.7 0.1 copy.22
  258.9 0.1 copy.21
  259.2 0.1 reshape.70
  259.3 96.2 %all-reduce.4.cloned.1.call-done = bf16[1024,2,896]{2,0,1:T(8,128)(2,1)} async-done(((bf16[1024,2,896]{2,0,1:T(8,128)(2,1)}), bf16[1024,2,896]{2,0,1:T(8,128)(2,1)}) %all-reduce.4.cloned.1.call-update) | async-done | bytes 3670032 | tf_op jit(solution)/shard_map/psum | solution.py:77
  355.5 2.5 convert_element_type.29
  358.0 2.3 fusion.3
  360.3 12.3 %gather_fusion.3 = bf16[2048,896]{1,0:T(8,128)(2,1)} fusion(bf16[1024,896]{1,0:T(8,128)(2,1)} %fusion.3, s32[2048]{0:T(1024)S(1)} %broadcast_clamp_fusion), kind=kCustom, calls=%fused_computation.3 | custom fusion | bytes 7348224 | tf_op jit(solution)/shard_map/gather | solution.py:82
  372.6 4.2 fusion.4
  376.7 0.1 broadcast_in_dim.54
  376.9 5.2 dynamic_update_slice.7
  382.0 86.1 %all-reduce.6 = bf16[64,32,64]{2,1,0:T(8,128)(2,1)S(1)} all-reduce(f32[64,32,64]{2,1,0:T(8,128)S(1)} %dynamic_update_slice.7), channel_id=1, replica_groups=mesh['rows'=8,'hidden'=32] {'rows','hidden'}, use_global_device_ids=true, to_apply=%region_6.7 | all-reduce | flops 131072 | bytes 786432 | tf_op jit(solution)/shard_map/psum | solution.py:91
  468.1 1.1 fusion.24
  469.2 3.3 scatter_custom_fusion
  472.5 6.4 %fusion.1 = bf16[1024,1024]{1,0:T(8,128)(2,1)} fusion(f32[1025,1024]{1,0:T(8,128)} %scatter_custom_fusion, bf16[1024,896]{1,0:T(8,128)(2,1)} %fusion.3, bf16[896,1024]{1,0:T(8,128)(2,1)S(1)} %copy-done), kind=kOutput, calls=%fused_computation.9 | convolution fusion | flops 1881145344 | bytes 9961472 | tf_op jit(solution)/shard_map/dot_general | solution.py:106
  478.9 85.7 %reduce-scatter.2.cloned.1.call-done = bf16[32,1024]{1,0:T(8,128)(2,1)} async-done(((bf16[1024,1024]{1,0:T(8,128)(2,1)}), bf16[32,1024]{1,0:T(8,128)(2,1)}) %reduce-scatter.2.cloned.1.call-update) | async-done | bytes 65552 | tf_op jit(solution)/shard_map/reduce_scatter | solution.py:104
  (36 shorter events, 0.6 us)
Async XLA Ops:
  6.5 466.0 %copy-start = (bf16[896,1024]{1,0:T(8,128)(2,1)S(1)}, bf16[896,1024]{1,0:T(8,128)(2,1)}, u32[]{:S(2)}) copy-start(bf16[896,1024]{1,0:T(8,128)(2,1)} %param.13) | copy-start | bytes 5505028
  6.5 57.5 %copy-start.5 = (bf16[2,1024,128]{2,1,0:T(8,128)(2,1)S(1)}, bf16[2,1024,128]{2,1,0:T(8,128)(2,1)}, u32[]{:S(2)}) copy-start(bf16[2,1024,128]{2,1,0:T(8,128)(2,1)} %param.14) | copy-start | bytes 1572868
  6.5 54.8 %all-gather.2.cloned.1.call-start = ((), (), s32[]{:S(2)}) async-start(), calls=%async_computation.1 | async-start | bytes 2162688 | tf_op jit(solution)/shard_map/all_gather | solution.py:50
  7.3 348.2 %all-reduce.4.cloned.1.call-start = ((), (), s32[]{:S(2)}) async-start(), calls=%async_computation.2 | async-start | bytes 7340032 | tf_op jit(solution)/shard_map/psum | solution.py:77
  199.2 5.5 copy-start.3
  248.5 4.6 copy-start.4
  248.5 4.6 copy-start.6
  253.2 2.3 copy-start.1
  253.2 3.2 copy-start.2
  258.5 306.1 %reduce-scatter.2.cloned.1.call-start = ((), (), s32[]{:S(2)}) async-start(), calls=%async_computation.3 | async-start | bytes 2162688 | tf_op jit(solution)/shard_map/reduce_scatter | solution.py:104
  360.3 12.3 %copy-start.7 = (bf16[64,8,896]{2,1,0:T(8,128)(2,1)S(1)}, bf16[64,8,896]{2,1,0:T(8,128)(2,1)}, u32[]{:S(2)}) copy-start(bf16[64,8,896]{2,1,0:T(8,128)(2,1)} %param.16) | copy-start | bytes 2752516
Sparse Core Ops, SparseCore 0:
  9.9 51.3 all-gather.1
  258.6 96.7 all-reduce.3
  479.0 85.4 reduce-scatter.1
where the time goes:
time: 572 us; the launch traced here: 571 us
  blocking collectives  217 us (38%)
  waiting for transfers between devices  210 us (37%)
  local copies, waits for them, and re-layouts  70.6 us (12%)
  other arithmetic  32.2 us (6%)
  matrix products  28.5 us (5%)
  between operations  13.3 us (2%)
    psum x1, blocking collectives, per_device(): rank_total = lax.psum(placed, ('rows', 'hidden'))  131 us
    psum x1, waiting for transfers between devices, per_device(): lax.psum((jnp.stack([gate_term, up_term], axis=1) + adapter_rows).astype(...  96.2 us
    psum x1, blocking collectives, per_device(): down_total = lax.psum(placed_down, ('rows', 'hidden'))  86.1 us
    reduce_scatter x1, waiting for transfers between devices, per_device(): lax.psum_scatter((jnp.dot(hidden_all, down_weight, preferred_element_type...  85.7 us
    gather x2, local copies, waits for them, and re-layouts, per_device(): halves.append(grouped_rows[snap_owner, slot_index])  39.7 us
    all_gather x1, waiting for transfers between devices, per_device(): gathered = lax.all_gather(tokens, 'hidden', axis=0, tiled=True)  26.9 us
    another operation x3, other arithmetic  18.2 us
    gather x1, local copies, waits for them, and re-layouts, per_device(): hidden_all[clamped_index]  12.3 us
  transfers between devices with their start and end apart: 3, of which 3 were waited for; matrix products, arithmetic and copies ran while one was open for 5% of the time, Pallas kernels for 0%

commit v1 on v0

--- a/solution.py
+++ b/solution.py
@@ -88,7 +88,7 @@
     placed_down = lax.dynamic_update_slice_in_dim(
         placed_down, down_part, row_index * rank_block_values, 2
     )
-    down_total = lax.psum(placed_down, ("rows", "hidden"))
+    down_total = lax.psum(lax.psum(placed_down, "rows"), "hidden")
     down_rank = lax.dynamic_slice_in_dim(down_total, own_first, snapshot_local, 0).astype(
         jnp.bfloat16
     )

time: 572 us -> 697 us (1.22)
  waiting for transfers between devices: 210 us -> 304 us
  blocking collectives: 217 us -> 247 us
    psum x0 -> x1, waiting for transfers between devices: none -> 81.7 us  [per_device(): down_total = lax.psum(lax.psum(placed_down, 'rows'), 'hidden')]
    psum x1, blocking collectives: 86.1 us -> 116 us  [per_device(): down_total = lax.psum(lax.psum(placed_down, 'rows'), 'hidden')]
    reduce_scatter x1, waiting for transfers between devices: 85.7 us -> 98.3 us  [per_device(): lax.psum_scatter((jnp.dot(hidden_all, down_weight, preferred_element_type...]
  transfers between devices with their start and end apart: 3 -> 4, of which waited for: 3 -> 4; matrix products, arithmetic and copies ran while one was open for 5% -> 4% of each run, Pallas kernels for 0% -> 0%
where the time goes in v1:
time: 697 us; the launch traced here: 696 us
  waiting for transfers between devices  304 us (44%)
  blocking collectives  247 us (35%)
  local copies, waits for them, and re-layouts  71.6 us (10%)
  other arithmetic  32.2 us (5%)
  matrix products  27.5 us (4%)
  between operations  13.4 us (2%)
    psum x1, blocking collectives, per_device(): rank_total = lax.psum(placed, ('rows', 'hidden'))  131 us
    psum x1, blocking collectives, per_device(): down_total = lax.psum(lax.psum(placed_down, 'rows'), 'hidden')  116 us
    reduce_scatter x1, waiting for transfers between devices, per_device(): lax.psum_scatter((jnp.dot(hidden_all, down_weight, preferred_element_type...  98.3 us
    psum x1, waiting for transfers between devices, per_device(): lax.psum((jnp.stack([gate_term, up_term], axis=1) + adapter_rows).astype(...  96.4 us
    psum x1, waiting for transfers between devices, per_device(): down_total = lax.psum(lax.psum(placed_down, 'rows'), 'hidden')  81.7 us
    gather x2, local copies, waits for them, and re-layouts, per_device(): halves.append(grouped_rows[snap_owner, slot_index])  39.7 us
    all_gather x1, waiting for transfers between devices, per_device(): gathered = lax.all_gather(tokens, 'hidden', axis=0, tiled=True)  26.9 us
    another operation x3, other arithmetic  18.2 us
  transfers between devices with their start and end apart: 4, of which 4 were waited for; matrix products, arithmetic and copies ran while one was open for 4% of the time, Pallas kernels for 0%

profile of v1, /device:TPU:2, one launch (start us, length us, event | category | flops | bytes accessed | tf_op | source)
XLA Modules:
  0.0 696.1 jit_solution(6537678002250859213)
XLA Ops:
  6.5 0.7 all-gather.2.cloned.1.call-update
  7.3 0.7 fusion.19
  8.0 18.0 %reduce-window.6 = s32[64,8,128]{2,1,0:T(8,128)S(1)} reduce-window(s32[64,8,128]{2,1,0:T(8,128)S(1)} %fusion.19, s32[]{:T(128)} %constant.16.clone.1), window={size=1x1x128 pad=0_0x0_0x127_0}, to_apply=%region_0.0 | reduce-window | flops 8323072 | bytes 524292 | tf_op jit(solution)/shard_map/reduce-window
  26.0 0.1 slice.44
  26.2 0.1 copy.13
  26.4 0.1 copy.14
  26.4 0.1 broadcast_add_fusion
  26.6 0.8 fusion.18
  27.3 0.7 shift-left_or_fusion
  28.1 0.7 multiply_reduce_fusion
  28.8 0.8 and_reduce_fusion
  29.6 4.3 scatter_custom_fusion.1
  34.1 0.1 reshape.78
  34.3 0.1 copy.15
  34.4 26.9 %all-gather.2.cloned.1.call-done = bf16[1024,1024]{1,0:T(8,128)(2,1)} async-done(((bf16[32,1024]{1,0:T(8,128)(2,1)}), bf16[1024,1024]{1,0:T(8,128)(2,1)}) %all-gather.2.cloned.1.call-update) | async-done | bytes 2097168 | tf_op jit(solution)/shard_map/all_gather | solution.py:50
  61.4 2.7 gather_fusion
  64.0 0.3 fusion.20
  64.3 0.1 reshape.69
  64.4 0.1 copy.17
  64.5 2.5 broadcast_in_dim.49
  67.0 0.6 constant_dynamic-update-slice_fusion
  67.6 130.6 %all-reduce.8 = bf16[64,32,2,64]{1,3,0,2:T(8,128)(2,1)} all-reduce(f32[64,32,2,64]{1,3,0,2:T(8,128)} %constant_dynamic-update-slice_fusion), channel_id=1, replica_groups=mesh['rows'=8,'hidden'=32] {'rows','hidden'}, use_global_device_ids=true, to_apply=%region_4.5 | all-reduce | flops 262144 | bytes 1572864 | tf_op jit(solution)/shard_map/psum | solution.py:60
  198.2 1.0 dynamic-slice_convert_fusion
  199.2 5.5 fusion.12
  204.7 4.1 fusion.10
  208.8 19.8 %gather_fusion.1 = f32[1024,896]{1,0:T(8,128)} fusion(f32[64,32,896]{2,1,0:T(8,128)} %fusion.12, s32[1024]{0:T(1024)S(1)} %bitcast.78), kind=kCustom, calls=%fused_computation.1 | custom fusion | bytes 7348224 | tf_op jit(solution)/shard_map/gather | solution.py:72
  228.7 19.9 %gather_fusion.2 = f32[1024,896]{1,0:T(8,128)} fusion(f32[64,32,896]{2,1,0:T(8,128)} %fusion.10, s32[1024]{0:T(1024)S(1)} %bitcast.79), kind=kCustom, calls=%fused_computation.2 | custom fusion | bytes 7348224 | tf_op jit(solution)/shard_map/gather | solution.py:72
  248.5 4.6 convolution_bitcast_fusion
  253.2 2.3 convolution_bitcast_fusion.1
  255.5 0.8 copy-done.2
  256.3 2.1 fusion
  258.5 0.2 all-reduce.7.cloned.1.call-start
  258.9 0.1 copy.21
  259.0 96.4 %all-reduce.5.cloned.1.call-done = bf16[1024,2,896]{2,0,1:T(8,128)(2,1)} async-done(((bf16[1024,2,896]{2,0,1:T(8,128)(2,1)}), bf16[1024,2,896]{2,0,1:T(8,128)(2,1)}) %all-reduce.5.cloned.1.call-update) | async-done | bytes 3670032 | tf_op jit(solution)/shard_map/psum | solution.py:77
  355.5 2.5 convert_element_type.29
  358.0 2.3 fusion.3
  360.3 12.3 %gather_fusion.3 = bf16[2048,896]{1,0:T(8,128)(2,1)} fusion(bf16[1024,896]{1,0:T(8,128)(2,1)} %fusion.3, s32[2048]{0:T(1024)S(1)} %broadcast_clamp_fusion), kind=kCustom, calls=%fused_computation.3 | custom fusion | bytes 7348224 | tf_op jit(solution)/shard_map/gather | solution.py:82
  372.6 4.2 fusion.4
  376.7 0.1 broadcast_in_dim.54
  376.9 5.2 dynamic_update_slice.7
  382.0 1.0 copy-done.3
  383.3 0.1 reshape.70
  383.4 81.7 %all-reduce.7.cloned.1.call-done = f32[64,32,64]{2,1,0:T(8,128)} async-done(((f32[64,32,64]{2,1,0:T(8,128)}), f32[64,32,64]{2,1,0:T(8,128)}) %all-reduce.7.cloned.1.call-update) | async-done | bytes 524304 | tf_op jit(solution)/shard_map/psum | solution.py:91
  465.1 116.2 %all-reduce.9 = bf16[64,32,64]{2,1,0:T(8,128)(2,1)S(1)} all-reduce(f32[64,32,64]{2,1,0:T(8,128)} %all-reduce.7.cloned.1.call-done), channel_id=1, replica_groups=mesh['rows'=8,'hidden'=32] {'hidden'}, use_global_device_ids=true, to_apply=%region_7.8 | all-reduce | flops 131072 | bytes 786432 | tf_op jit(solution)/shard_map/psum | solution.py:91
  581.3 0.2 fusion.24
  581.5 3.3 scatter_custom_fusion
  584.8 6.4 fusion.1
  591.2 98.3 %reduce-scatter.2.cloned.1.call-done = bf16[32,1024]{1,0:T(8,128)(2,1)} async-done(((bf16[1024,1024]{1,0:T(8,128)(2,1)}), bf16[32,1024]{1,0:T(8,128)(2,1)}) %reduce-scatter.2.cloned.1.call-update) | async-done | bytes 65552 | tf_op jit(solution)/shard_map/reduce_scatter | solution.py:104
  (43 shorter events, 0.9 us)
Async XLA Ops:
  6.5 578.2 %copy-start = (bf16[896,1024]{1,0:T(8,128)(2,1)S(1)}, bf16[896,1024]{1,0:T(8,128)(2,1)}, u32[]{:S(2)}) copy-start(bf16[896,1024]{1,0:T(8,128)(2,1)} %param.13) | copy-start | bytes 5505028
  6.5 57.5 %copy-start.6 = (bf16[2,1024,128]{2,1,0:T(8,128)(2,1)S(1)}, bf16[2,1024,128]{2,1,0:T(8,128)(2,1)}, u32[]{:S(2)}) copy-start(bf16[2,1024,128]{2,1,0:T(8,128)(2,1)} %param.14) | copy-start | bytes 1572868
  6.5 54.8 %all-gather.2.cloned.1.call-start = ((), (), s32[]{:S(2)}) async-start(), calls=%async_computation.1 | async-start | bytes 2162688 | tf_op jit(solution)/shard_map/all_gather | solution.py:50
  7.3 348.2 %all-reduce.5.cloned.1.call-start = ((), (), s32[]{:S(2)}) async-start(), calls=%async_computation.2 | async-start | bytes 7340032 | tf_op jit(solution)/shard_map/psum | solution.py:77
  199.2 5.5 copy-start.4
  248.5 4.6 copy-start.5
  248.5 4.6 copy-start.8
  253.2 2.3 copy-start.1
  253.2 3.2 copy-start.2
  258.5 206.6 %all-reduce.7.cloned.1.call-start = ((), (), s32[]{:S(2)}) async-start(), calls=%async_computation.3 | async-start | bytes 2097152 | tf_op jit(solution)/shard_map/psum | solution.py:91
  360.3 12.3 %copy-start.9 = (bf16[64,8,896]{2,1,0:T(8,128)(2,1)S(1)}, bf16[64,8,896]{2,1,0:T(8,128)(2,1)}, u32[]{:S(2)}) copy-start(bf16[64,8,896]{2,1,0:T(8,128)(2,1)} %param.16) | copy-start | bytes 2752516
  376.7 204.6 %copy-start.7 = (bf16[2,64,1024]{2,1,0:T(8,128)(2,1)S(1)}, bf16[2,64,1024]{2,1,0:T(8,128)(2,1)}, u32[]{:S(2)}) copy-start(bf16[2,64,1024]{2,1,0:T(8,128)(2,1)} %param.17) | copy-start | bytes 786436
  382.0 1.0 copy-start.3
  383.1 306.5 %reduce-scatter.2.cloned.1.call-start = ((), (), s32[]{:S(2)}) async-start(), calls=%async_computation.4 | async-start | bytes 2162688 | tf_op jit(solution)/shard_map/reduce_scatter | solution.py:104
Sparse Core Ops, SparseCore 0:
  9.9 51.3 all-gather.1
  258.6 96.8 all-reduce.4
  383.2 81.8 all-reduce.6
  591.3 98.1 reduce-scatter.1
